TPU v7x, 32 devices: a whole 2x2x4 slice. The times are simulated.
32 devices in a mesh: dp: 2 (over x), orient: 16 (over z, y, core).
Axes of the slice: x: 2, y: 2, z: 4, core: 2. Of those that a mesh axis runs over, the one named last changes fastest.
Arguments:
- images: bfloat16 [384, 16384], P(('dp', 'orient')), may hold values from -80 to 80
- templates: bfloat16 [4096, 16384], P('orient'), as said below
- index: int32 [4096, 128], P('orient'), may hold values from 0 to 16383
- interp: float32 [4096, 128], P('orient'), may hold values from 0.25 to 1
- inv_noise: float32 [128, 128], replicated, may hold values from 0.5 to 2, as said below
Outputs:
- recon: float32 [16384, 128], P(('dp', 'orient'))
- recon_weight: float32 [16384, 128], P(('dp', 'orient'))
Inputs may be any that keep to these rules, and one draw needn't show every extreme that they name: `templates`: every entry has magnitude at most 18 / 128. `inv_noise`: every entry is 0.5, 1 or 2.
All inputs are finite; a program needn't handle non-finite values.
Results may differ from a plain program's by a relative error of at most 0.0029.
Values may be sent and summed in bfloat16 or wider, within the bound.
A program may use at most 128 MiB of HBM per device.

v0:
```python
import jax
import jax.numpy as jnp
from jax import lax
from jax.sharding import PartitionSpec as P


def shards(images, templates, index, interp, inv_noise):
    side = inv_noise.shape[0]
    count_tpl = templates.shape[0]
    noise_flat = inv_noise.reshape(-1)
    tpl_f = templates.astype(jnp.float32)
    weighted = (tpl_f * noise_flat[None, :]).astype(jnp.bfloat16)
    tnorm = 0.5 * jnp.sum(tpl_f * tpl_f * noise_flat[None, :], axis=1)
    gathered = lax.all_gather(images, "orient", axis=0, tiled=True)
    scores = (
        lax.dot_general(
            gathered, weighted, (((1,), (1,)), ((), ())), preferred_element_type=jnp.float32
        )
        - tnorm[None, :]
    )
    peak = lax.pmax(jnp.max(scores, axis=1), "orient")
    expo = jnp.exp(scores - peak[:, None])
    total = lax.psum(jnp.sum(expo, axis=1), "orient")
    posterior = expo / total[:, None]
    post_b = posterior.astype(jnp.bfloat16)
    mass = jnp.sum(posterior, axis=0)
    sums = lax.dot_general(
        post_b, gathered, (((0,), (0,)), ((), ())), preferred_element_type=jnp.float32
    )
    rows_idx = index.reshape(-1)
    data_rows = sums.reshape(count_tpl * side, side) * interp.reshape(-1, 1)
    data_vol = jnp.zeros((side * side, side), jnp.float32).at[rows_idx].add(data_rows)
    weight_rows = ((interp * mass[:, None])[:, :, None] * inv_noise[None, :, :]).reshape(
        count_tpl * side, side
    )
    weight_vol = jnp.zeros((side * side, side), jnp.float32).at[rows_idx].add(weight_rows)
    volume = jnp.concatenate([data_vol, weight_vol], axis=1)
    owned = lax.psum_scatter(volume, ("dp", "orient"), scatter_dimension=0, tiled=True)
    return (owned[:, :side], owned[:, side:])


def solution(mesh):
    placed = (
        P(("dp", "orient"), None),
        P("orient", None),
        P("orient", None),
        P("orient", None),
        P(),
    )
    return jax.shard_map(
        shards,
        mesh=mesh,
        in_specs=placed,
        out_specs=(P(("dp", "orient"), None), P(("dp", "orient"), None)),
        check_vma=False,
    )
```

profile of v0, /device:TPU:0, one launch (start us, length us, event | category | flops | bytes accessed | tf_op | source)
XLA Modules:
  0.0 777.0 jit_solution(3466400453175574872)
XLA Ops:
  7.2 0.0 copy-start.1
  7.2 0.0 all-gather.3.cloned.1.call-start
  7.2 0.7 all-gather.3.cloned.1.call-update
  7.9 0.0 reduce-scatter.2.cloned.1.call-start
  8.0 5.7 fusion.2
  13.6 1.0 compare_select_fusion
  14.7 73.1 %all-gather.3.cloned.1.call-done = bf16[16,12,16384]{2,1,0:T(8,128)(2,1)} async-done(((bf16[1,12,16384]{2,1,0:T(8,128)(2,1)}), bf16[16,12,16384]{2,1,0:T(8,128)(2,1)}) %all-gather.3.cloned.1.call-update) | async-done | bytes 6291472 | tf_op jit(solution)/shard_map/all_gather | solution.py:14
  87.8 8.8 %reshape.72 = bf16[192,16384]{1,0:T(8,128)(2,1)} reshape(bf16[16,12,16384]{2,1,0:T(8,128)(2,1)} %all-gather.3.cloned.1.call-done) | data formatting | bytes 12582912
  96.6 0.0 copy-done.1
  96.6 8.2 %fusion.22 = (f32[192]{0:T(256)S(1)}, f32[256,192]{0,1:T(8,128)S(1)}) fusion(f32[256]{0:T(256)S(1)} %broadcast_multiply_fusion, bf16[192,16384]{1,0:T(8,128)(2,1)} %reshape.72, bf16[256,16384]{1,0:T(8,128)(2,1)} %param.6, f32[16384]{0:T(1024)S(1)} %bitcast.14), kind=kOutput, calls=%fused_computation.28 | convolution fusion | flops 1623293696 | bytes 14944000 | tf_op jit(solution)/shard_map/dot_general | solution.py:16
  104.8 31.0 %pmax.7 = f32[192]{0:T(256)S(1)} all-reduce(f32[192]{0:T(256)S(1)} %get-tuple-element.4), channel_id=1, replica_groups=mesh['dp'=2,'orient'=16] {'orient'}, use_global_device_ids=true, to_apply=%region_2.0 | all-reduce | flops 192 | bytes 1536 | tf_op jit(solution)/shard_map/pmax | solution.py:21
  135.7 0.2 fusion.16
  135.9 29.5 %psum.7 = f32[192]{0:T(256)S(1)} all-reduce(f32[192]{0:T(256)S(1)} %fusion.16), channel_id=1, replica_groups=mesh['dp'=2,'orient'=16] {'orient'}, use_global_device_ids=true, to_apply=%region_4.0 | all-reduce | flops 192 | bytes 1536 | tf_op jit(solution)/shard_map/psum | solution.py:23
  165.4 11.0 %fusion.17 = f32[256,16384]{1,0:T(8,128)} fusion(bf16[192,16384]{1,0:T(8,128)(2,1)} %reshape.72, f32[256,192]{0,1:T(8,128)S(1)} %get-tuple-element.5, f32[192]{0:T(256)S(1)} %psum.7, f32[192]{0:T(256)S(1)} %pmax.7), kind=kOutput, calls=%fused_computation.23 | convolution fusion | flops 1610760192 | bytes 23266816 | tf_op jit(solution)/shard_map/dot_general | solution.py:27
  176.4 0.1 fusion.19
  176.6 18.1 %reshape.54 = f32[32768,128]{1,0:T(8,128)} reshape(f32[256,16384]{1,0:T(8,128)} %fusion.17) | data formatting | bytes 33554432 | tf_op jit(solution)/shard_map/reshape | solution.py:31
  194.6 0.1 multiply_bitcast_fusion
  194.7 8.5 %bitcast_multiply_fusion = f32[32768,128]{1,0:T(8,128)} fusion(f32[128,128]{1,0:T(8,128)S(1)} %copy-done.1, f32[32768]{0:T(1024)S(1)} %multiply_bitcast_fusion), kind=kLoop, calls=%fused_computation.8 | loop fusion | flops 4194304 | bytes 16973824 | tf_op jit(solution)/shard_map/mul | solution.py:33
  203.2 177.9 %scatter_custom_fusion.1 = f32[16384,128]{1,0:T(8,128)} fusion(s32[32768]{0:T(1024)S(1)} %bitcast.16, f32[32768,128]{1,0:T(8,128)} %bitcast_multiply_fusion, f32[]{:T(128)} %constant.5.clone.1), kind=kCustom, calls=%fused_computation.14 | custom fusion | flops 4194304 | bytes 8389120 | tf_op jit(solution)/shard_map/scatter-add | solution.py:36
  381.1 194.9 %scatter_custom_fusion = f32[16384,128]{1,0:T(8,128)} fusion(s32[32768]{0:T(1024)S(1)} %bitcast.17, f32[32768,128]{1,0:T(8,128)} %reshape.54, f32[32768]{0:T(1024)S(1)} %bitcast.11, f32[]{:T(128)} %constant.5.clone.1), kind=kCustom, calls=%fused_computation.9 | custom fusion | flops 8388608 | bytes 25296900 | tf_op jit(solution)/shard_map/scatter-add | solution.py:32
  576.0 11.3 %pad_maximum_fusion = f32[16384,256]{1,0:T(8,128)} fusion(f32[16384,128]{1,0:T(8,128)} %scatter_custom_fusion.1, f32[16384,128]{1,0:T(8,128)} %scatter_custom_fusion), kind=kLoop, calls=%fused_computation.7 | loop fusion | flops 4194304 | bytes 33554432 | tf_op jit(solution)/shard_map/concatenate | solution.py:37
  587.3 0.0 reduce-scatter.2.cloned.1.call-update
  587.3 181.0 %reduce-scatter.2.cloned.1.call-done = f32[512,256]{1,0:T(8,128)} async-done(((f32[16384,256]{1,0:T(8,128)}), f32[512,256]{1,0:T(8,128)}) %reduce-scatter.2.cloned.1.call-update) | async-done | bytes 524304 | tf_op jit(solution)/shard_map/reduce_scatter | solution.py:38
  768.3 1.9 fusion.21
  (3 shorter events, 0.0 us)
Async XLA Ops:
  7.2 89.4 %copy-start.1 = (f32[128,128]{1,0:T(8,128)S(1)}, f32[128,128]{1,0:T(8,128)}, u32[]{:S(2)}) copy-start(f32[128,128]{1,0:T(8,128)} %param.9) | copy-start | bytes 196612
  7.2 80.6 %all-gather.3.cloned.1.call-start = ((), (), s32[]{:S(2)}) async-start(), calls=%async_computation.2 | async-start | bytes 8912896 | tf_op jit(solution)/shard_map/all_gather | solution.py:14
  7.9 760.4 %reduce-scatter.2.cloned.1.call-start = ((), (), s32[]{:S(2)}) async-start(), calls=%async_computation.1 | async-start | bytes 17301504 | tf_op jit(solution)/shard_map/reduce_scatter | solution.py:38
  176.6 18.1 %copy-start = (f32[256,128]{1,0:T(8,128)S(1)}, f32[256,128]{1,0:T(8,128)}, u32[]{:S(2)}) copy-start(f32[256,128]{1,0:T(8,128)} %param.8) | copy-start | bytes 393220
Sparse Core Ops, SparseCore 0:
  10.2 77.5 all-gather.2
  587.4 180.8 reduce-scatter.1
where the time goes:
time: 778 us; the launch traced here: 777 us
  other arithmetic  400 us (51%)
  waiting for transfers between devices  255 us (33%)
  blocking collectives  60.5 us (8%)
  local copies, waits for them, and re-layouts  28.7 us (4%)
  matrix products  19.2 us (2%)
  between operations  14.1 us (2%)
    scatter-add x1, other arithmetic, shards(): jnp.zeros((side * side, side), jnp.float32).at[rows_idx].add(data_rows)  195 us
    reduce_scatter x1, waiting for transfers between devices, shards(): lax.psum_scatter(volume, ('dp', 'orient'), scatter_dimension=0, tiled=True)  181 us
    scatter-add x1, other arithmetic, shards(): jnp.zeros((side * side, side), jnp.float32).at[rows_idx].add(weight_rows)  178 us
    all_gather x1, waiting for transfers between devices, shards(): gathered = lax.all_gather(images, 'orient', axis=0, tiled=True)  73.1 us
    pmax x1, blocking collectives, shards(): peak = lax.pmax(jnp.max(scores, axis=1), 'orient')  31 us
    psum x1, blocking collectives, shards(): total = lax.psum(jnp.sum(expo, axis=1), 'orient')  29.5 us
    reshape x1, local copies, waits for them, and re-layouts, shards(): data_rows = sums.reshape(count_tpl * side, side) * interp.reshape(-1, 1)  18.1 us
  transfers between devices with their start and end apart: 2, of which 2 were waited for; matrix products, arithmetic and copies ran while one was open for 1% of the time, Pallas kernels for 0%

commit v1 on v0

--- a/solution.py
+++ b/solution.py
@@ -2,6 +2,27 @@
 import jax.numpy as jnp
 from jax import lax
 from jax.sharding import PartitionSpec as P
+
+
+def ring_gather(x, axis, dim):
+    devices, index, rows = (lax.axis_size(axis), lax.axis_index(axis), x.shape[dim])
+    ahead = [(i, (i + 1) % devices) for i in range(devices)]
+    backward = [(i, (i - 1) % devices) for i in range(devices)]
+    out = jnp.zeros((*x.shape[:dim], devices * rows, *x.shape[dim + 1 :]), x.dtype)
+    out = lax.dynamic_update_slice_in_dim(out, x, index * rows, axis=dim)
+    from_left = from_right = x
+    half = devices // 2
+    for step in range(1, half + 1):
+        from_left = lax.ppermute(from_left, axis, ahead)
+        out = lax.dynamic_update_slice_in_dim(
+            out, from_left, (index - step) % devices * rows, axis=dim
+        )
+        if step < devices - half:
+            from_right = lax.ppermute(from_right, axis, backward)
+            out = lax.dynamic_update_slice_in_dim(
+                out, from_right, (index + step) % devices * rows, axis=dim
+            )
+    return out
 
 
 def shards(images, templates, index, interp, inv_noise):
@@ -11,7 +32,7 @@
     tpl_f = templates.astype(jnp.float32)
     weighted = (tpl_f * noise_flat[None, :]).astype(jnp.bfloat16)
     tnorm = 0.5 * jnp.sum(tpl_f * tpl_f * noise_flat[None, :], axis=1)
-    gathered = lax.all_gather(images, "orient", axis=0, tiled=True)
+    gathered = ring_gather(images, "orient", 0)
     scores = (
         lax.dot_general(
             gathered, weighted, (((1,), (1,)), ((), ())), preferred_element_type=jnp.float32

time: 778 us -> 873 us (1.12)
  starting transfers between devices: 0.08 us -> 68.6 us
  local copies, waits for them, and re-layouts: 28.7 us -> 96.9 us
  waiting for transfers between devices: 255 us -> 211 us
    dynamic_update_slice x0 -> x16, local copies, waits for them, and re-layouts: none -> 73.6 us  [the longest x8 36.2 us: ring_gather(): lax.dynamic_update_slice_in_dim(out, from_left, (index - step) % devices...]
    all_gather x1 -> x0, waiting for transfers between devices: 73.1 us -> none  [shards(): gathered = lax.all_gather(images, 'orient', axis=0, tiled=True)]
    ppermute x0 -> x15, starting transfers between devices: none -> 68.5 us  [the longest x8 61.3 us: ring_gather(): from_left = lax.ppermute(from_left, axis, ahead)]
    ppermute x0 -> x15, waiting for transfers between devices: none -> 29.4 us  [the longest x8 29.4 us: ring_gather(): from_left = lax.ppermute(from_left, axis, ahead)]
    unnamed x5 -> x24, local copies, waits for them, and re-layouts: 8.79 us -> 0.05 us
  transfers between devices with their start and end apart: 2 -> 16, of which waited for: 2 -> 8; matrix products, arithmetic and copies ran while one was open for 1% -> 9% of each run, Pallas kernels for 0% -> 0%
where the time goes in v1:
time: 873 us; the launch traced here: 871 us
  other arithmetic  400 us (46%)
  waiting for transfers between devices  211 us (24%)
  local copies, waits for them, and re-layouts  96.9 us (11%)
  starting transfers between devices  68.6 us (8%)
  blocking collectives  61.7 us (7%)
  matrix products  19.2 us (2%)
  between operations  14.4 us (2%)
    scatter-add x1, other arithmetic, shards(): jnp.zeros((side * side, side), jnp.float32).at[rows_idx].add(data_rows)  195 us
    reduce_scatter x1, waiting for transfers between devices, shards(): lax.psum_scatter(volume, ('dp', 'orient'), scatter_dimension=0, tiled=True)  181 us
    scatter-add x1, other arithmetic, shards(): jnp.zeros((side * side, side), jnp.float32).at[rows_idx].add(weight_rows)  178 us
    ppermute x8, starting transfers between devices, ring_gather(): from_left = lax.ppermute(from_left, axis, ahead)  61.3 us
    dynamic_update_slice x8, local copies, waits for them, and re-layouts, ring_gather(): lax.dynamic_update_slice_in_dim(out, from_left, (index - step) % devices...  36.2 us
    dynamic_update_slice x7, local copies, waits for them, and re-layouts, ring_gather(): lax.dynamic_update_slice_in_dim(out, from_right, (index + step) % devices...  32.8 us
    pmax x1, blocking collectives, shards(): peak = lax.pmax(jnp.max(scores, axis=1), 'orient')  32.1 us
    psum x1, blocking collectives, shards(): total = lax.psum(jnp.sum(expo, axis=1), 'orient')  29.7 us
  transfers between devices with their start and end apart: 16, of which 8 were waited for; matrix products, arithmetic and copies ran while one was open for 9% of the time, Pallas kernels for 0%

profile of v1, /device:TPU:0, one launch (start us, length us, event | category | flops | bytes accessed | tf_op | source)
XLA Modules:
  0.0 870.9 jit_solution(8499730739675813631)
XLA Ops:
  7.7 5.1 collective-permute-start.1
  12.8 7.1 collective-permute-done
  24.4 6.9 collective-permute-done.2
  35.9 6.8 collective-permute-done.4
  42.7 6.6 collective-permute-start.6
  54.0 9.5 %collective-permute-start.8 = (bf16[12,16384]{1,0:T(8,128)(2,1)S(1)}, bf16[12,16384]{1,0:T(8,128)(2,1)S(1)}, u32[]{:S(2)}, u32[]{:S(2)}) collective-permute-start(bf16[12,16384]{1,0:T(8,128)(2,1)S(1)} %collective-permute-done.6), channel_id=1, source_target_pairs={{0,1},{1,2},{2,3},{3,4},{4,5},{5,6},{6,7},{7,8},{8,9},{9,10},{10,1... | collective-permute-start | bytes 1179656 | tf_op jit(solution)/shard_map/ppermute | solution.py:16
  65.4 12.3 %collective-permute-start.10 = (bf16[12,16384]{1,0:T(8,128)(2,1)S(1)}, bf16[12,16384]{1,0:T(8,128)(2,1)S(1)}, u32[]{:S(2)}, u32[]{:S(2)}) collective-permute-start(bf16[12,16384]{1,0:T(8,128)(2,1)S(1)} %collective-permute-done.8), channel_id=1, source_target_pairs={{0,1},{1,2},{2,3},{3,4},{4,5},{5,6},{6,7},{7,8},{8,9},{9,10},{10,1... | collective-permute-start | bytes 1179656 | tf_op jit(solution)/shard_map/ppermute | solution.py:16
  79.3 12.7 %collective-permute-start.12 = (bf16[12,16384]{1,0:T(8,128)(2,1)S(1)}, bf16[12,16384]{1,0:T(8,128)(2,1)}, u32[]{:S(2)}, u32[]{:S(2)}) collective-permute-start(bf16[12,16384]{1,0:T(8,128)(2,1)S(1)} %collective-permute-done.10), channel_id=1, source_target_pairs={{0,1},{1,2},{2,3},{3,4},{4,5},{5,6},{6,7},{7,8},{8,9},{9,10},{10,1... | collective-permute-start | bytes 1179656 | tf_op jit(solution)/shard_map/ppermute | solution.py:16
  93.7 12.6 %collective-permute-start.14 = (bf16[12,16384]{1,0:T(8,128)(2,1)}, bf16[12,16384]{1,0:T(8,128)(2,1)}, u32[]{:S(2)}, u32[]{:S(2)}) collective-permute-start(bf16[12,16384]{1,0:T(8,128)(2,1)} %collective-permute-done.12), channel_id=1, source_target_pairs={{0,1},{1,2},{2,3},{3,4},{4,5},{5,6},{6,7},{7,8},{8,9},{9,10},{10,1... | collective-permute-start | bytes 1179656 | tf_op jit(solution)/shard_map/ppermute | solution.py:16
  106.2 5.7 fusion.2
  146.8 4.8 dynamic_update_slice.55
  151.6 4.8 dynamic_update_slice.56
  179.6 4.8 dynamic_update_slice.62
  184.4 4.8 dynamic_update_slice.63
  189.2 8.2 fusion.22
  197.4 32.1 %pmax.7 = f32[192]{0:T(256)S(1)} all-reduce(f32[192]{0:T(256)S(1)} %get-tuple-element.4), channel_id=1, replica_groups=mesh['dp'=2,'orient'=16] {'orient'}, use_global_device_ids=true, to_apply=%region_2.3 | all-reduce | flops 192 | bytes 1536 | tf_op jit(solution)/shard_map/pmax | solution.py:42
  229.6 29.7 %psum.7 = f32[192]{0:T(256)S(1)} all-reduce(f32[192]{0:T(256)S(1)} %fusion.16), channel_id=1, replica_groups=mesh['dp'=2,'orient'=16] {'orient'}, use_global_device_ids=true, to_apply=%region_4.5 | all-reduce | flops 192 | bytes 1536 | tf_op jit(solution)/shard_map/psum | solution.py:44
  259.3 11.0 %fusion.17 = f32[256,16384]{1,0:T(8,128)} fusion(bf16[192,16384]{1,0:T(8,128)(2,1)} %dynamic_update_slice.63, f32[192,256]{1,0:T(8,128)S(1)} %get-tuple-element.5, f32[192]{0:T(256)S(1)} %psum.7, f32[192]{0:T(256)S(1)} %pmax.7), kind=kOutput, calls=%fused_computation.23 | convolution fusion | flops 1610760192 | bytes 23266816 | tf_op jit(solution)/shard_map/dot_general | solution.py:48
  270.4 18.0 %reshape.54 = f32[32768,128]{1,0:T(8,128)} reshape(f32[256,16384]{1,0:T(8,128)} %fusion.17) | data formatting | bytes 33554432 | tf_op jit(solution)/shard_map/reshape | solution.py:52
  288.6 8.4 bitcast_multiply_fusion
  297.0 177.9 %scatter_custom_fusion.1 = f32[16384,128]{1,0:T(8,128)} fusion(s32[32768]{0:T(1024)S(1)} %bitcast.14, f32[32768,128]{1,0:T(8,128)} %bitcast_multiply_fusion, f32[]{:T(128)} %constant.95.clone.1), kind=kCustom, calls=%fused_computation.14 | custom fusion | flops 4194304 | bytes 8389120 | tf_op jit(solution)/shard_map/scatter-add | solution.py:57
  474.9 194.9 %scatter_custom_fusion = f32[16384,128]{1,0:T(8,128)} fusion(s32[32768]{0:T(1024)S(1)} %bitcast.15, f32[32768,128]{1,0:T(8,128)} %reshape.54, f32[32768]{0:T(1024)S(1)} %bitcast.10, f32[]{:T(128)} %constant.95.clone.1), kind=kCustom, calls=%fused_computation.9 | custom fusion | flops 8388608 | bytes 25296900 | tf_op jit(solution)/shard_map/scatter-add | solution.py:53
  669.8 11.3 %pad_maximum_fusion = f32[16384,256]{1,0:T(8,128)} fusion(f32[16384,128]{1,0:T(8,128)} %scatter_custom_fusion.1, f32[16384,128]{1,0:T(8,128)} %scatter_custom_fusion), kind=kLoop, calls=%fused_computation.7 | loop fusion | flops 4194304 | bytes 33554432 | tf_op jit(solution)/shard_map/concatenate | solution.py:58
  681.1 181.1 %reduce-scatter.2.cloned.1.call-done = f32[512,256]{1,0:T(8,128)} async-done(((f32[16384,256]{1,0:T(8,128)}), f32[512,256]{1,0:T(8,128)}) %reduce-scatter.2.cloned.1.call-update) | async-done | bytes 524304 | tf_op jit(solution)/shard_map/reduce_scatter | solution.py:59
  (66 shorter events, 79.4 us)
Async XLA Ops:
  7.2 108.3 %copy-start.1 = (bf16[12,16384]{1,0:T(8,128)(2,1)S(1)}, bf16[12,16384]{1,0:T(8,128)(2,1)}, u32[]{:S(2)}) copy-start(bf16[12,16384]{1,0:T(8,128)(2,1)} %param.5) | copy-start | bytes 1179652
  7.2 855.1 %reduce-scatter.2.cloned.1.call-start = ((), (), s32[]{:S(2)}) async-start(), calls=%async_computation.1 | async-start | bytes 17301504 | tf_op jit(solution)/shard_map/reduce_scatter | solution.py:59
  7.2 12.7 %collective-permute-start = (bf16[12,16384]{1,0:T(8,128)(2,1)}, bf16[12,16384]{1,0:T(8,128)(2,1)S(1)}, u32[]{:S(2)}, u32[]{:S(2)}) collective-permute-start(bf16[12,16384]{1,0:T(8,128)(2,1)} %param.5), channel_id=1, source_target_pairs={{0,1},{1,2},{2,3},{3,4},{4,5},{5,6},{6,7},{7,8},{8,9},{9,10},{10,1... | collective-permute-start | bytes 1179656 | tf_op jit(solution)/shard_map/ppermute | solution.py:16
  7.7 14.7 %collective-permute-start.1 = (bf16[12,16384]{1,0:T(8,128)(2,1)}, bf16[12,16384]{1,0:T(8,128)(2,1)S(1)}, u32[]{:S(2)}, u32[]{:S(2)}) collective-permute-start(bf16[12,16384]{1,0:T(8,128)(2,1)} %param.5), channel_id=1, source_target_pairs={{0,15},{1,0},{2,1},{3,2},{4,3},{5,4},{6,5},{7,6},{8,7},{9,8},{10,9... | collective-permute-start | bytes 1179656 | tf_op jit(solution)/shard_map/ppermute | solution.py:21
  19.9 11.4 %collective-permute-start.2 = (bf16[12,16384]{1,0:T(8,128)(2,1)S(1)}, bf16[12,16384]{1,0:T(8,128)(2,1)S(1)}, u32[]{:S(2)}, u32[]{:S(2)}) collective-permute-start(bf16[12,16384]{1,0:T(8,128)(2,1)S(1)} %collective-permute-done), channel_id=1, source_target_pairs={{0,1},{1,2},{2,3},{3,4},{4,5},{5,6},{6,7},{7,8},{8,9},{9,10},{10,1... | collective-permute-start | bytes 1179656 | tf_op jit(solution)/shard_map/ppermute | solution.py:16
  22.4 13.5 %collective-permute-start.3 = (bf16[12,16384]{1,0:T(8,128)(2,1)S(1)}, bf16[12,16384]{1,0:T(8,128)(2,1)S(1)}, u32[]{:S(2)}, u32[]{:S(2)}) collective-permute-start(bf16[12,16384]{1,0:T(8,128)(2,1)S(1)} %collective-permute-done.1), channel_id=1, source_target_pairs={{0,15},{1,0},{2,1},{3,2},{4,3},{5,4},{6,5},{7,6},{8,7},{9,8},{10,9... | collective-permute-start | bytes 1179656 | tf_op jit(solution)/shard_map/ppermute | solution.py:21
  31.3 11.4 %collective-permute-start.4 = (bf16[12,16384]{1,0:T(8,128)(2,1)S(1)}, bf16[12,16384]{1,0:T(8,128)(2,1)S(1)}, u32[]{:S(2)}, u32[]{:S(2)}) collective-permute-start(bf16[12,16384]{1,0:T(8,128)(2,1)S(1)} %collective-permute-done.2), channel_id=1, source_target_pairs={{0,1},{1,2},{2,3},{3,4},{4,5},{5,6},{6,7},{7,8},{8,9},{9,10},{10,1... | collective-permute-start | bytes 1179656 | tf_op jit(solution)/shard_map/ppermute | solution.py:16
  35.9 13.5 %collective-permute-start.5 = (bf16[12,16384]{1,0:T(8,128)(2,1)S(1)}, bf16[12,16384]{1,0:T(8,128)(2,1)S(1)}, u32[]{:S(2)}, u32[]{:S(2)}) collective-permute-start(bf16[12,16384]{1,0:T(8,128)(2,1)S(1)} %collective-permute-done.3), channel_id=1, source_target_pairs={{0,15},{1,0},{2,1},{3,2},{4,3},{5,4},{6,5},{7,6},{8,7},{9,8},{10,9... | collective-permute-start | bytes 1179656 | tf_op jit(solution)/shard_map/ppermute | solution.py:21
  42.7 11.3 %collective-permute-start.6 = (bf16[12,16384]{1,0:T(8,128)(2,1)S(1)}, bf16[12,16384]{1,0:T(8,128)(2,1)S(1)}, u32[]{:S(2)}, u32[]{:S(2)}) collective-permute-start(bf16[12,16384]{1,0:T(8,128)(2,1)S(1)} %collective-permute-done.4), channel_id=1, source_target_pairs={{0,1},{1,2},{2,3},{3,4},{4,5},{5,6},{6,7},{7,8},{8,9},{9,10},{10,1... | collective-permute-start | bytes 1179656 | tf_op jit(solution)/shard_map/ppermute | solution.py:16
  49.3 14.2 %collective-permute-start.7 = (bf16[12,16384]{1,0:T(8,128)(2,1)S(1)}, bf16[12,16384]{1,0:T(8,128)(2,1)S(1)}, u32[]{:S(2)}, u32[]{:S(2)}) collective-permute-start(bf16[12,16384]{1,0:T(8,128)(2,1)S(1)} %collective-permute-done.5), channel_id=1, source_target_pairs={{0,15},{1,0},{2,1},{3,2},{4,3},{5,4},{6,5},{7,6},{8,7},{9,8},{10,9... | collective-permute-start | bytes 1179656 | tf_op jit(solution)/shard_map/ppermute | solution.py:21
  54.0 11.4 %collective-permute-start.8 = (bf16[12,16384]{1,0:T(8,128)(2,1)S(1)}, bf16[12,16384]{1,0:T(8,128)(2,1)S(1)}, u32[]{:S(2)}, u32[]{:S(2)}) collective-permute-start(bf16[12,16384]{1,0:T(8,128)(2,1)S(1)} %collective-permute-done.6), channel_id=1, source_target_pairs={{0,1},{1,2},{2,3},{3,4},{4,5},{5,6},{6,7},{7,8},{8,9},{9,10},{10,1... | collective-permute-start | bytes 1179656 | tf_op jit(solution)/shard_map/ppermute | solution.py:16
  63.6 14.2 %collective-permute-start.9 = (bf16[12,16384]{1,0:T(8,128)(2,1)S(1)}, bf16[12,16384]{1,0:T(8,128)(2,1)S(1)}, u32[]{:S(2)}, u32[]{:S(2)}) collective-permute-start(bf16[12,16384]{1,0:T(8,128)(2,1)S(1)} %collective-permute-done.7), channel_id=1, source_target_pairs={{0,15},{1,0},{2,1},{3,2},{4,3},{5,4},{6,5},{7,6},{8,7},{9,8},{10,9... | collective-permute-start | bytes 1179656 | tf_op jit(solution)/shard_map/ppermute | solution.py:21
  65.4 12.4 %copy-start.5 = (bf16[12,16384]{1,0:T(8,128)(2,1)}, bf16[12,16384]{1,0:T(8,128)(2,1)S(1)}, u32[]{:S(2)}) copy-start(bf16[12,16384]{1,0:T(8,128)(2,1)S(1)} %collective-permute-done.8) | copy-start | bytes 1179652
  65.4 13.9 %collective-permute-start.10 = (bf16[12,16384]{1,0:T(8,128)(2,1)S(1)}, bf16[12,16384]{1,0:T(8,128)(2,1)S(1)}, u32[]{:S(2)}, u32[]{:S(2)}) collective-permute-start(bf16[12,16384]{1,0:T(8,128)(2,1)S(1)} %collective-permute-done.8), channel_id=1, source_target_pairs={{0,1},{1,2},{2,3},{3,4},{4,5},{5,6},{6,7},{7,8},{8,9},{9,10},{10,1... | collective-permute-start | bytes 1179656 | tf_op jit(solution)/shard_map/ppermute | solution.py:16
  77.8 15.3 %collective-permute-start.11 = (bf16[12,16384]{1,0:T(8,128)(2,1)S(1)}, bf16[12,16384]{1,0:T(8,128)(2,1)}, u32[]{:S(2)}, u32[]{:S(2)}) collective-permute-start(bf16[12,16384]{1,0:T(8,128)(2,1)S(1)} %collective-permute-done.9), channel_id=1, source_target_pairs={{0,15},{1,0},{2,1},{3,2},{4,3},{5,4},{6,5},{7,6},{8,7},{9,8},{10,9... | collective-permute-start | bytes 1179656 | tf_op jit(solution)/shard_map/ppermute | solution.py:21
  79.3 13.7 %copy-start.9 = (bf16[12,16384]{1,0:T(8,128)(2,1)}, bf16[12,16384]{1,0:T(8,128)(2,1)S(1)}, u32[]{:S(2)}) copy-start(bf16[12,16384]{1,0:T(8,128)(2,1)S(1)} %collective-permute-done.10) | copy-start | bytes 1179652
  79.3 14.4 %collective-permute-start.12 = (bf16[12,16384]{1,0:T(8,128)(2,1)S(1)}, bf16[12,16384]{1,0:T(8,128)(2,1)}, u32[]{:S(2)}, u32[]{:S(2)}) collective-permute-start(bf16[12,16384]{1,0:T(8,128)(2,1)S(1)} %collective-permute-done.10), channel_id=1, source_target_pairs={{0,1},{1,2},{2,3},{3,4},{4,5},{5,6},{6,7},{7,8},{8,9},{9,10},{10,1... | collective-permute-start | bytes 1179656 | tf_op jit(solution)/shard_map/ppermute | solution.py:16
  93.1 86.5 %collective-permute-start.13 = (bf16[12,16384]{1,0:T(8,128)(2,1)}, bf16[12,16384]{1,0:T(8,128)(2,1)}, u32[]{:S(2)}, u32[]{:S(2)}) collective-permute-start(bf16[12,16384]{1,0:T(8,128)(2,1)} %collective-permute-done.11), channel_id=1, source_target_pairs={{0,15},{1,0},{2,1},{3,2},{4,3},{5,4},{6,5},{7,6},{8,7},{9,8},{10,9... | collective-permute-start | bytes 1179656 | tf_op jit(solution)/shard_map/ppermute | solution.py:21
  93.7 90.7 %collective-permute-start.14 = (bf16[12,16384]{1,0:T(8,128)(2,1)}, bf16[12,16384]{1,0:T(8,128)(2,1)}, u32[]{:S(2)}, u32[]{:S(2)}) collective-permute-start(bf16[12,16384]{1,0:T(8,128)(2,1)} %collective-permute-done.12), channel_id=1, source_target_pairs={{0,1},{1,2},{2,3},{3,4},{4,5},{5,6},{6,7},{7,8},{8,9},{9,10},{10,1... | collective-permute-start | bytes 1179656 | tf_op jit(solution)/shard_map/ppermute | solution.py:16
  115.5 73.7 %copy-start.11 = (f32[128,128]{1,0:T(8,128)S(1)}, f32[128,128]{1,0:T(8,128)}, u32[]{:S(2)}) copy-start(f32[128,128]{1,0:T(8,128)} %param.9) | copy-start | bytes 196612
  120.1 36.3 %copy-start.6 = (bf16[12,16384]{1,0:T(8,128)(2,1)S(1)}, bf16[12,16384]{1,0:T(8,128)(2,1)}, u32[]{:S(2)}) copy-start(bf16[12,16384]{1,0:T(8,128)(2,1)} %copy-done.5) | copy-start | bytes 1179652
  123.7 37.2 %copy-start.8 = (bf16[12,16384]{1,0:T(8,128)(2,1)S(1)}, bf16[12,16384]{1,0:T(8,128)(2,1)}, u32[]{:S(2)}) copy-start(bf16[12,16384]{1,0:T(8,128)(2,1)} %copy-done.7) | copy-start | bytes 1179652
  128.3 37.1 %copy-start.10 = (bf16[12,16384]{1,0:T(8,128)(2,1)S(1)}, bf16[12,16384]{1,0:T(8,128)(2,1)}, u32[]{:S(2)}) copy-start(bf16[12,16384]{1,0:T(8,128)(2,1)} %copy-done.9) | copy-start | bytes 1179652
  270.4 18.0 %copy-start = (f32[256,128]{1,0:T(8,128)S(1)}, f32[256,128]{1,0:T(8,128)}, u32[]{:S(2)}) copy-start(f32[256,128]{1,0:T(8,128)} %param.8) | copy-start | bytes 393220
  (4 other events, 17.6 us)
Sparse Core Ops, SparseCore 0:
  681.2 180.9 reduce-scatter.1
